TPU v7x, 32 devices: a whole 2x2x4 slice. The times are simulated.
32 devices in a mesh: row: 16 (over z, y, core), col: 2 (over x).
Axes of the slice: x: 2, y: 2, z: 4, core: 2. Of those that a mesh axis runs over, the one named last changes fastest.
Arguments:
- object_field: bfloat16 [2, 4096, 2048], P(None, 'row', 'col'), may hold values from -6 to 6
- probe: float32 [2, 2, 256, 256], replicated, may hold values from -5 to 5
- measured: bfloat16 [16, 2, 12, 256, 256], P('row', 'col'), may hold values from 0.3984375 to 4
- positions: int32 [16, 2, 12, 2], P('row', 'col'), may hold values from 0 to 1023, as said below
- counts: int32 [16, 2], P('row', 'col'), may hold values from 1 to 12, as said below
Outputs:
- object_grad: float32 [2, 4096, 2048], P(None, 'row', 'col')
- probe_grad: float32 [2, 2, 256, 256], replicated
Inputs may be any that keep to these rules, and one draw needn't show every extreme that they name: positions[i, j, s, 0] lies in 0 to 255 and positions[i, j, s, 1] in 0 to 1023 for every slot, live or not. `counts`: some tile has all 12 slots live.
All inputs are finite; a program needn't handle non-finite values.
Results may differ from a plain program's by a relative error of at most 0.0048.
The roundings to bfloat16 on the way count: a program that leaves them out, or rounds other values in their place, can miss the bound.
Values may be sent and summed in bfloat16 or wider, within the bound.
A program may use at most 128 MiB of HBM per device.

v0:
```python
import functools

import jax
import jax.numpy as jnp
import numpy as np
from jax import lax
from jax.experimental import pallas as pl
from jax.experimental.pallas import tpu as pltpu
from jax.sharding import PartitionSpec as P

MESH = pl.DeviceIdType.MESH
LANES = 128
CHUNK = 64
F32 = jnp.float32
BF16 = jnp.bfloat16


def dft_blocks(size):
    index = np.arange(size)
    angle = 2.0 * np.pi / size * (index[:, None] * index[None, :] % size)
    cosine = np.cos(angle) / np.sqrt(size)
    sine = np.sin(angle) / np.sqrt(size)
    one = np.block([[cosine, sine], [-sine, cosine]])
    other = np.block([[cosine, -sine], [sine, cosine]])
    return jnp.asarray(one, F32).astype(BF16), jnp.asarray(other, F32).astype(BF16)


def dot(a, b):
    return jnp.dot(a, b, preferred_element_type=F32)


def work_kernel(
    pos_ref, count_ref, own_ref, below_ref, strip_ref, corner_ref, frames_ref, probe_ref, one_ref, other_ref,
    grad_ref, band_ref, side_ref, edge_ref, sum_ref,
    ext, acc, patch, wave, half, weighted, half2,
):
    rows, cols = own_ref.shape[1:]
    size = probe_ref.shape[-1]
    high, blocks = rows + size, (cols + size) // LANES

    def line(plane, block, row):
        return (plane * blocks + block) * high + row

    for c in range(2):
        for block in range(blocks):
            at = block * LANES
            inside = at < cols
            at = at if inside else at - cols
            top, bottom = (own_ref, below_ref) if inside else (strip_ref, corner_ref)
            ext[pl.ds(line(c, block, 0), rows), :] = top[c, :, at : at + LANES].astype(F32)
            ext[pl.ds(line(c, block, rows), size), :] = bottom[c, :, at : at + LANES].astype(F32)
    acc[...] = jnp.zeros_like(acc)
    sum_ref[...] = jnp.zeros_like(sum_ref)
    per = size // LANES
    lane = lax.broadcasted_iota(jnp.int32, (CHUNK, LANES), 1)

    @pl.loop(0, count_ref[0])
    def _(slot):
        row = pos_ref[2 * slot]
        col = pos_ref[2 * slot + 1]
        first = col // LANES
        shift = col - first * LANES
        back_shift = lax.rem(LANES - shift, LANES)
        low = lane < LANES - shift
        high_lanes = lane >= shift
        for start in range(0, size, CHUNK):
            rs = pl.ds(start, CHUNK)
            obj = []
            for c in range(2):
                turned = [
                    pltpu.roll(ext[pl.ds(line(c, first + b, row + start), CHUNK), :], back_shift, 1)
                    for b in range(per + 1)
                ]
                value = jnp.concatenate([jnp.where(low, turned[b], turned[b + 1]) for b in range(per)], 1)
                patch[c, rs, :] = value
                obj.append(value)
            re, im = obj
            for m in range(2):
                pre, pim = probe_ref[m, 0, rs, :], probe_ref[m, 1, rs, :]
                ms = pl.ds(m * size, size)
                wave[rs, ms] = (pre * re - pim * im).astype(BF16)
                wave[pl.ds(size + start, CHUNK), ms] = (pre * im + pim * re).astype(BF16)
        for o in range(2):
            os = pl.ds(o * size, size)
            out = dot(one_ref[os, :], wave[...])
            for m in range(2):
                half[pl.ds(m * size, size), os] = out[:, m * size : (m + 1) * size].astype(BF16)
        for start in range(0, size, 2 * CHUNK):
            spec = [dot(half[pl.ds(m * size + start, 2 * CHUNK), :], other_ref[...]) for m in range(2)]
            for sub in range(0, 2 * CHUNK, CHUNK):
                s = [v[sub : sub + CHUNK] for v in spec]
                square = [v[:, :size] * v[:, :size] + v[:, size:] * v[:, size:] for v in s]
                inv = lax.rsqrt(square[0] + square[1] + 1.0)
                rs = pl.ds(start + sub, CHUNK)
                factor = 1.0 - frames_ref[slot, rs, :].astype(F32) * inv
                for m in range(2):
                    for d in range(2):
                        part = s[m][:, d * size : (d + 1) * size] * factor
                        weighted[pl.ds(d * size + start + sub, CHUNK), pl.ds(m * size, size)] = part.astype(BF16)
        for o in range(2):
            os = pl.ds(o * size, size)
            out = dot(other_ref[os, :], weighted[...])
            for m in range(2):
                half2[pl.ds(m * size, size), os] = out[:, m * size : (m + 1) * size].astype(BF16)
        for start in range(0, size, 2 * CHUNK):
            back = [dot(half2[pl.ds(m * size + start, 2 * CHUNK), :], one_ref[...]) for m in range(2)]
            for sub in range(0, 2 * CHUNK, CHUNK):
                at = start + sub
                rs = pl.ds(at, CHUNK)
                ore, oim = patch[0, rs, :], patch[1, rs, :]
                gre = gim = None
                for m in range(2):
                    bre = back[m][sub : sub + CHUNK, :size]
                    bim = back[m][sub : sub + CHUNK, size:]
                    pre, pim = probe_ref[m, 0, rs, :], probe_ref[m, 1, rs, :]
                    a = pre * bre + pim * bim
                    b = pre * bim - pim * bre
                    gre, gim = (a, b) if m == 0 else (gre + a, gim + b)
                    qre = ore * bre + oim * bim
                    qim = ore * bim - oim * bre
                    for d, q in enumerate((qre, qim)):
                        for h in range(size // LANES):
                            block = (m * 2 + d) * (size // LANES) + h
                            sum_ref[pl.ds(block * size + at, CHUNK), :] += q[:, h * LANES : (h + 1) * LANES]
                nothing = jnp.zeros((CHUNK, LANES), F32)
                for c, g in enumerate((gre, gim)):
                    turned = [pltpu.roll(g[:, b * LANES : (b + 1) * LANES], shift, 1) for b in range(per)]
                    turned = [nothing] + turned + [nothing]
                    for b in range(per + 1):
                        here = pl.ds(line(c, first + b, row + at), CHUNK)
                        acc[here, :] += jnp.where(high_lanes, turned[b + 1], turned[b])

    for c in range(2):
        for block in range(blocks):
            at = block * LANES
            inside = at < cols
            at = at if inside else at - cols
            upper = acc[pl.ds(line(c, block, 0), rows), :]
            lower = acc[pl.ds(line(c, block, rows), size), :].astype(BF16)
            if inside:
                grad_ref[c, :, at : at + LANES] = upper
                band_ref[c, :, at : at + LANES] = lower
            else:
                side_ref[c, :, at : at + LANES] = upper.astype(BF16)
                edge_ref[c, :, at : at + LANES] = lower


def join_kernel(
    n_row, n_col, scale,
    grad_ref, band_ref, side_ref, edge_ref, sum_ref,
    out_ref, probe_ref,
    band_in, side_in, edge_in, send1, recv1, acc, send2, recv2, acc2, recv3, full2, full1, wide, send_sem, recv_sem,
):
    i, j = lax.axis_index("row"), lax.axis_index("col")
    size2, size3 = 2 * n_col, n_row // 4
    k = lax.rem(i, 2)
    g2 = lax.rem(i // 2, 2) * n_col + j
    g3 = i // 4
    n1 = sum_ref.shape[0] // 2
    n2 = n1 // size2
    n3 = n2 // size3
    partner = (i + 1 - 2 * k, j)

    def peer2(d):
        p = lax.rem(g2 + d, size2)
        return (g3 * 4 + p // n_col * 2 + k, lax.rem(p, n_col))

    def peer3(d):
        return (lax.rem(g3 + d, size3) * 4 + lax.rem(i, 4), j)

    has_down, has_up, has_right, has_left = i < n_row - 1, i > 0, j < n_col - 1, j > 0
    sides = (
        (has_down, has_up, (i + 1, j), (i - 1, j), band_ref, band_in),
        (has_right, has_left, (i, j + 1), (i, j - 1), side_ref, side_in),
        (has_down & has_right, has_up & has_left, (i + 1, j + 1), (i - 1, j - 1), edge_ref, edge_in),
    )
    barrier = pltpu.get_barrier_semaphore()
    peers = [partner] + [peer2(d) for d in range(1, size2)] + [peer3(d) for d in range(1, size3)]
    for peer in peers:
        pl.semaphore_signal(barrier, inc=1, device_id=peer, device_id_type=MESH)
    for _, gets, _, source, _, _ in sides:

        @pl.when(gets)
        def _():
            pl.semaphore_signal(barrier, inc=1, device_id=source, device_id_type=MESH)

    targets = sum(sends.astype(jnp.int32) for sends, _, _, _, _, _ in sides)
    pl.semaphore_wait(barrier, len(peers) + targets)

    used = [0]

    def copy(src, dst, to):
        at = used[0]
        used[0] += 1
        return pltpu.make_async_remote_copy(
            src_ref=src, dst_ref=dst, send_sem=send_sem.at[at], recv_sem=recv_sem.at[at], device_id=to, device_id_type=MESH
        )

    send1[...] = sum_ref[pl.ds(pl.multiple_of((1 - k) * n1, n1), n1), :].astype(BF16)
    first = copy(send1, recv1, partner)
    first.start()
    side_copies = []
    for sends, gets, to, _, src, dst in sides:
        c = copy(src, dst, to)
        side_copies.append(c)

        @pl.when(sends)
        def _():
            c.start()

    first.wait()
    total = sum_ref[pl.ds(pl.multiple_of(k * n1, n1), n1), :] + recv1[...].astype(F32)
    acc[...] = total
    send2[...] = total.astype(BF16).reshape(send2.shape)
    second = [copy(send2.at[lax.rem(g2 + d, size2)], recv2.at[d - 1], peer2(d)) for d in range(1, size2)]
    for c in second:
        c.start()
    total = acc[pl.ds(pl.multiple_of(g2 * n2, n2), n2), :]
    for d, c in enumerate(second):
        c.wait()
        total = total + recv2[d].astype(F32)
    acc2[...] = total.reshape(acc2.shape)
    third = [copy(acc2.at[lax.rem(g3 + d, size3)], recv3.at[d - 1], peer3(d)) for d in range(1, size3)]
    for c in third:
        c.start()
    total = acc2[g3]
    for d, c in enumerate(third):
        c.wait()
        total = total + recv3[d]
    full2[g3] = total * scale
    third = [copy(full2.at[g3], full2.at[g3], peer3(d)) for d in range(1, size3)]
    for c in third:
        c.start()
    for c in third:
        c.wait()
    full1[g2] = full2[...].reshape(n2, LANES).astype(BF16)
    second = [copy(full1.at[g2], full1.at[g2], peer2(d)) for d in range(1, size2)]
    for c in second:
        c.start()
    for c in second:
        c.wait()
    wide[k] = full1[...].reshape(n1, LANES)
    last = copy(wide.at[k], wide.at[k], partner)
    last.start()
    out_ref[...] = grad_ref[...]
    rows, cols = out_ref.shape[1:]
    size = probe_ref.shape[-1]
    for (sends, gets, _, _, _, dst), c in zip(sides, side_copies):
        span = dst.shape[2]

        @pl.when(gets)
        def _():
            c.wait_recv()
            out_ref[:, :, :span] += dst[...].astype(F32)

        @pl.when(sends)
        def _():
            c.wait_send()

    last.wait()
    per = size // LANES
    for block in range(4 * per):
        part = wide[block * size // n1, pl.ds(block * size % n1, size), :]
        mode, plane, h = block // (2 * per), block // per % 2, block % per
        probe_ref[mode, plane, :, h * LANES : (h + 1) * LANES] = part.astype(F32)


def body(n_row, n_col, object_field, probe, measured, positions, counts):
    size = probe.shape[-1]
    rows, cols = object_field.shape[1:]
    slots = measured.shape[2]
    one, other = dft_blocks(size)
    head = object_field[:, :, :size]
    below = lax.ppermute(object_field, "row", [(i + 1, i) for i in range(n_row - 1)])
    strip = lax.ppermute(head, "col", [(j + 1, j) for j in range(n_col - 1)])
    diagonal = [
        ((i + 1) * n_col + j + 1, i * n_col + j) for i in range(n_row - 1) for j in range(n_col - 1)
    ]
    corner = lax.ppermute(head, ("row", "col"), diagonal)
    vmem = pl.BlockSpec(memory_space=pltpu.VMEM)
    smem = pl.BlockSpec(memory_space=pltpu.SMEM)
    lines = 4 * size * size // LANES
    work = pl.pallas_call(
        work_kernel,
        out_shape=[
            jax.ShapeDtypeStruct((2, rows, cols), F32),
            jax.ShapeDtypeStruct((2, size, cols), BF16),
            jax.ShapeDtypeStruct((2, rows, size), BF16),
            jax.ShapeDtypeStruct((2, size, size), BF16),
            jax.ShapeDtypeStruct((lines, LANES), F32),
        ],
        in_specs=[smem, smem] + [vmem] * 8,
        out_specs=[vmem] * 5,
        scratch_shapes=[
            pltpu.VMEM((2 * (rows + size) * (cols + size) // LANES, LANES), F32),
            pltpu.VMEM((2 * (rows + size) * (cols + size) // LANES, LANES), F32),
            pltpu.VMEM((2, size, size), F32),
        ]
        + [pltpu.VMEM((2 * size, 2 * size), BF16)] * 4,
        compiler_params=pltpu.CompilerParams(vmem_limit_bytes=48 * 2**20),
        name="scan",
    )
    grad, band, side, edge, total = work(
        positions.reshape(-1), counts.reshape(-1), object_field, below, strip, corner, measured[0, 0], probe, one, other
    )
    size2, size3 = 2 * n_col, n_row // 4
    n1 = lines // 2
    n2 = n1 // size2
    n3 = n2 // size3
    n_copies = 2 + 3 + 2 * (size2 - 1) + 2 * (size3 - 1)
    join = pl.pallas_call(
        functools.partial(join_kernel, n_row, n_col, 1.0 / float(np.sqrt(slots * n_row * n_col))),
        out_shape=[
            jax.ShapeDtypeStruct((2, rows, cols), F32),
            jax.ShapeDtypeStruct(probe.shape, F32),
        ],
        in_specs=[vmem] * 5,
        out_specs=[vmem] * 2,
        scratch_shapes=[
            pltpu.VMEM(band.shape, BF16),
            pltpu.VMEM(side.shape, BF16),
            pltpu.VMEM(edge.shape, BF16),
            pltpu.VMEM((n1, LANES), BF16),
            pltpu.VMEM((n1, LANES), BF16),
            pltpu.VMEM((n1, LANES), F32),
            pltpu.VMEM((size2, n2, LANES), BF16),
            pltpu.VMEM((size2 - 1, n2, LANES), BF16),
            pltpu.VMEM((size3, n3, LANES), F32),
            pltpu.VMEM((size3 - 1, n3, LANES), F32),
            pltpu.VMEM((size3, n3, LANES), F32),
            pltpu.VMEM((size2, n2, LANES), BF16),
            pltpu.VMEM((2, n1, LANES), BF16),
            pltpu.SemaphoreType.DMA((n_copies,)),
            pltpu.SemaphoreType.DMA((n_copies,)),
        ],
        compiler_params=pltpu.CompilerParams(
            collective_id=0, has_side_effects=True, vmem_limit_bytes=40 * 2**20
        ),
        name="join",
    )
    return tuple(join(grad, band, side, edge, total))


def solution(mesh):
    placed = (
        P(None, "row", "col"),
        P(),
        P("row", "col", None, None, None),
        P("row", "col", None, None),
        P("row", "col"),
    )
    return jax.shard_map(
        functools.partial(body, mesh.shape["row"], mesh.shape["col"]),
        mesh=mesh,
        in_specs=placed,
        out_specs=(P(None, "row", "col"), P()),
        check_vma=False,
    )
```

profile of v0, /device:TPU:17, one launch (start us, length us, event | category | flops | bytes accessed | tf_op | source)
XLA Modules:
  0.0 90.1 jit_solution(7903148749933392875)
XLA Ops:
  0.6 2.6 %collective-permute-start = (bf16[2,256,1024]{2,1,0:T(8,128)(2,1)}, bf16[2,256,1024]{2,1,0:T(8,128)(2,1)S(1)}, u32[]{:S(2)}, u32[]{:S(2)}) collective-permute-start(bf16[2,256,1024]{2,1,0:T(8,128)(2,1)} %own_ref.1), channel_id=1, source_target_pairs={{2,0},{4,2},{6,4},{8,6},{10,8},{12,10},{14,12},{16,14},{18,16},{20... | collective-permute-start | bytes 3145736 | tf_op jit(solution)/shard_map/ppermute | solution.py:274
  3.2 1.0 %slice.3 = bf16[2,256,256]{2,1,0:T(8,128)(2,1)S(1)} slice(bf16[2,256,1024]{2,1,0:T(8,128)(2,1)} %own_ref.1), slice={[0:2], [0:256], [0:256]} | slice | bytes 524288 | tf_op jit(solution)/shard_map/slice | solution.py:273
  4.2 1.3 %collective-permute-start.2 = (bf16[2,256,256]{2,1,0:T(8,128)(2,1)S(1)}, bf16[2,256,256]{2,1,0:T(8,128)(2,1)S(1)}, u32[]{:S(2)}, u32[]{:S(2)}) collective-permute-start(bf16[2,256,256]{2,1,0:T(8,128)(2,1)S(1)} %slice.3), channel_id=1, source_target_pairs={{3,0},{5,2},{7,4},{9,6},{11,8},{13,10},{15,12},{17,14},{19,16},{21... | collective-permute-start | bytes 786440 | tf_op jit(solution)/shard_map/ppermute | solution.py:279
  5.5 1.3 %collective-permute-start.1 = (bf16[2,256,256]{2,1,0:T(8,128)(2,1)S(1)}, bf16[2,256,256]{2,1,0:T(8,128)(2,1)S(1)}, u32[]{:S(2)}, u32[]{:S(2)}) collective-permute-start(bf16[2,256,256]{2,1,0:T(8,128)(2,1)S(1)} %slice.3), channel_id=1, source_target_pairs={{1,0},{3,2},{5,4},{7,6},{9,8},{11,10},{13,12},{15,14},{17,16},{19,... | collective-permute-start | bytes 786440 | tf_op jit(solution)/shard_map/ppermute | solution.py:275
  7.4 0.8 copy.10
  8.2 0.1 reshape.10.pos_ref
  8.3 7.2 %collective-permute-done.2.corner_ref = bf16[2,256,256]{2,1,0:T(8,128)(2,1)S(1)} collective-permute-done((bf16[2,256,256]{2,1,0:T(8,128)(2,1)S(1)}, bf16[2,256,256]{2,1,0:T(8,128)(2,1)S(1)}, u32[]{:S(2)}, u32[]{:S(2)}) %collective-permute-start.2) | collective-permute-done | bytes 262176 | tf_op jit(solution)/shard_map/ppermute | solution.py:279
  15.5 2.1 %collective-permute-done.1.strip_ref = bf16[2,256,256]{2,1,0:T(8,128)(2,1)S(1)} collective-permute-done((bf16[2,256,256]{2,1,0:T(8,128)(2,1)S(1)}, bf16[2,256,256]{2,1,0:T(8,128)(2,1)S(1)}, u32[]{:S(2)}, u32[]{:S(2)}) %collective-permute-start.1) | collective-permute-done | bytes 262176 | tf_op jit(solution)/shard_map/ppermute | solution.py:275
  17.7 2.2 %collective-permute-done.below_ref = bf16[2,256,1024]{2,1,0:T(8,128)(2,1)S(1)} collective-permute-done((bf16[2,256,1024]{2,1,0:T(8,128)(2,1)}, bf16[2,256,1024]{2,1,0:T(8,128)(2,1)S(1)}, u32[]{:S(2)}, u32[]{:S(2)}) %collective-permute-start) | collective-permute-done | bytes 1048608 | tf_op jit(solution)/shard_map/ppermute | solution.py:274
  19.8 0.0 copy-start.4
  19.8 1.0 %copy-done.4 = bf16[2,256,1024]{2,1,0:T(8,128)(2,1)} copy-done((bf16[2,256,1024]{2,1,0:T(8,128)(2,1)}, bf16[2,256,1024]{2,1,0:T(8,128)(2,1)S(1)}, u32[]{:S(2)}) %copy-start.4) | copy-done | bytes 1048600
  20.8 0.0 copy-start.1
  20.8 1.2 %copy-done.1 = bf16[2,256,1024]{2,1,0:T(8,128)(2,1)S(1)} copy-done((bf16[2,256,1024]{2,1,0:T(8,128)(2,1)S(1)}, bf16[2,256,1024]{2,1,0:T(8,128)(2,1)}, u32[]{:S(2)}) %copy-start.1) | copy-done | bytes 1048600
  22.0 0.0 copy-start.2
  22.0 1.0 %copy-done.2 = bf16[512,512]{1,0:T(8,128)(2,1)S(1)} copy-done((bf16[512,512]{1,0:T(8,128)(2,1)S(1)}, bf16[512,512]{1,0:T(8,128)(2,1)}, u32[]{:S(2)}) %copy-start.2) | copy-done | bytes 524312
  23.1 0.0 copy-start.3
  23.1 1.0 %copy-done.3 = bf16[512,512]{1,0:T(8,128)(2,1)S(1)} copy-done((bf16[512,512]{1,0:T(8,128)(2,1)S(1)}, bf16[512,512]{1,0:T(8,128)(2,1)}, u32[]{:S(2)}) %copy-start.3) | copy-done | bytes 524312
  24.1 8.6 %scan.1 = (f32[2,256,1024]{2,1,0:T(8,128)}, bf16[2,256,1024]{2,1,0:T(8,128)(2,1)S(1)}, bf16[2,256,256]{2,1,0:T(8,128)(2,1)S(1)}, bf16[2,256,256]{2,1,0:T(8,128)(2,1)S(1)}, f32[2048,128]{1,0:T(8,128)S(1)}) custom-call(s32[24]{0:T(128)S(1)} %reshape.10.pos_ref, s32[1]{0:T(128)} %bitcast.2.count_ref, bf16[2,256,1024]{2,1,0:T(8,128)(2,1)S(1)} %copy-done.1, ...), custom_call_target="tpu_custom_call" | custom-call | tf_op jit(solution)/shard_map/scan/pallas_call | solution.py:303
  32.8 0.0 copy-start
  32.8 1.6 %copy-done = f32[2,256,1024]{2,1,0:T(8,128)S(1)} copy-done((f32[2,256,1024]{2,1,0:T(8,128)S(1)}, f32[2,256,1024]{2,1,0:T(8,128)}, u32[]{:S(2)}) %copy-start) | copy-done | bytes 2097176
  34.4 53.5 %join.1 = (f32[2,256,1024]{2,1,0:T(8,128)S(1)}, f32[2,2,256,256]{3,2,1,0:T(8,128)S(1)}) custom-call(f32[2,256,1024]{2,1,0:T(8,128)S(1)} %copy-done, bf16[2,256,1024]{2,1,0:T(8,128)(2,1)S(1)} %get-tuple-element.8.band_ref, bf16[2,256,256]{2,1,0:T(8,128)(2,1)S(1)} %get-tuple-element.9.side_ref, bf16[2,256,256]{2,1,0:T(8,128)(2,1)S(1)} %get-tuple-element.10.edge_ref, ...), custom_call_target="tpu_custom_call" | custom-call | tf_op jit(solution)/shard_map/join/pallas_call | solution.py:341
  87.8 1.3 %copy.14 = f32[2,256,1024]{2,1,0:T(8,128)} copy(f32[2,256,1024]{2,1,0:T(8,128)S(1)} %get-tuple-element.14) | data formatting | bytes 4194304
  89.2 1.0 %copy.15 = f32[2,2,256,256]{3,2,1,0:T(8,128)} copy(f32[2,2,256,256]{3,2,1,0:T(8,128)S(1)} %get-tuple-element.15) | data formatting | bytes 2097152
Async XLA Ops:
  0.6 19.2 %collective-permute-start = (bf16[2,256,1024]{2,1,0:T(8,128)(2,1)}, bf16[2,256,1024]{2,1,0:T(8,128)(2,1)S(1)}, u32[]{:S(2)}, u32[]{:S(2)}) collective-permute-start(bf16[2,256,1024]{2,1,0:T(8,128)(2,1)} %own_ref.1), channel_id=1, source_target_pairs={{2,0},{4,2},{6,4},{8,6},{10,8},{12,10},{14,12},{16,14},{18,16},{20... | collective-permute-start | bytes 3145736 | tf_op jit(solution)/shard_map/ppermute | solution.py:274
  4.2 11.3 %collective-permute-start.2 = (bf16[2,256,256]{2,1,0:T(8,128)(2,1)S(1)}, bf16[2,256,256]{2,1,0:T(8,128)(2,1)S(1)}, u32[]{:S(2)}, u32[]{:S(2)}) collective-permute-start(bf16[2,256,256]{2,1,0:T(8,128)(2,1)S(1)} %slice.3), channel_id=1, source_target_pairs={{3,0},{5,2},{7,4},{9,6},{11,8},{13,10},{15,12},{17,14},{19,16},{21... | collective-permute-start | bytes 786440 | tf_op jit(solution)/shard_map/ppermute | solution.py:279
  5.5 12.2 %collective-permute-start.1 = (bf16[2,256,256]{2,1,0:T(8,128)(2,1)S(1)}, bf16[2,256,256]{2,1,0:T(8,128)(2,1)S(1)}, u32[]{:S(2)}, u32[]{:S(2)}) collective-permute-start(bf16[2,256,256]{2,1,0:T(8,128)(2,1)S(1)} %slice.3), channel_id=1, source_target_pairs={{1,0},{3,2},{5,4},{7,6},{9,8},{11,10},{13,12},{15,14},{17,16},{19,... | collective-permute-start | bytes 786440 | tf_op jit(solution)/shard_map/ppermute | solution.py:275
  19.8 1.0 %copy-start.4 = (bf16[2,256,1024]{2,1,0:T(8,128)(2,1)}, bf16[2,256,1024]{2,1,0:T(8,128)(2,1)S(1)}, u32[]{:S(2)}) copy-start(bf16[2,256,1024]{2,1,0:T(8,128)(2,1)S(1)} %collective-permute-done.below_ref) | copy-start | bytes 3145732
  20.8 1.2 %copy-start.1 = (bf16[2,256,1024]{2,1,0:T(8,128)(2,1)S(1)}, bf16[2,256,1024]{2,1,0:T(8,128)(2,1)}, u32[]{:S(2)}) copy-start(bf16[2,256,1024]{2,1,0:T(8,128)(2,1)} %own_ref.1) | copy-start | bytes 3145732
  22.0 1.0 %copy-start.2 = (bf16[512,512]{1,0:T(8,128)(2,1)S(1)}, bf16[512,512]{1,0:T(8,128)(2,1)}, u32[]{:S(2)}) copy-start(bf16[512,512]{1,0:T(8,128)(2,1)} %constant.10.other_ref) | copy-start | bytes 1572868
  23.1 1.0 %copy-start.3 = (bf16[512,512]{1,0:T(8,128)(2,1)S(1)}, bf16[512,512]{1,0:T(8,128)(2,1)}, u32[]{:S(2)}) copy-start(bf16[512,512]{1,0:T(8,128)(2,1)} %constant.9.one_ref) | copy-start | bytes 1572868
  32.8 1.6 %copy-start = (f32[2,256,1024]{2,1,0:T(8,128)S(1)}, f32[2,256,1024]{2,1,0:T(8,128)}, u32[]{:S(2)}) copy-start(f32[2,256,1024]{2,1,0:T(8,128)} %get-tuple-element.7.grad_ref) | copy-start | bytes 6291460
where the time goes:
time: 90.3 us; the launch traced here: 90.1 us
  Pallas kernels  62.1 us (69%)
  waiting for transfers between devices  11.5 us (13%)
  local copies, waits for them, and re-layouts  9.98 us (11%)
  starting transfers between devices  5.17 us (6%)
  between operations  1.32 us (1%)
    pallas_call x1, Pallas kernels, body(): return tuple(join(grad, band, side, edge, total))  53.5 us
    unnamed x13, local copies, waits for them, and re-layouts  8.93 us
    pallas_call x1, Pallas kernels, body(): work(positions.reshape(-1), counts.reshape(-1), object_field, below, stri...  8.65 us
    ppermute x1, waiting for transfers between devices, body(): corner = lax.ppermute(head, ('row', 'col'), diagonal)  7.24 us
    ppermute x1, starting transfers between devices, body(): lax.ppermute(object_field, 'row', [(i + 1, i) for i in range(n_row - 1)])  2.59 us
    ppermute x1, waiting for transfers between devices, body(): lax.ppermute(object_field, 'row', [(i + 1, i) for i in range(n_row - 1)])  2.17 us
    ppermute x1, waiting for transfers between devices, body(): strip = lax.ppermute(head, 'col', [(j + 1, j) for j in range(n_col - 1)])  2.13 us
  transfers between devices with their start and end apart: 3, of which 3 were waited for; matrix products, arithmetic and copies ran while one was open for 2% of the time, Pallas kernels for 0%

commit v1 on v0

--- a/solution.py
+++ b/solution.py
@@ -32,7 +32,7 @@
 def work_kernel(
     pos_ref, count_ref, own_ref, below_ref, strip_ref, corner_ref, frames_ref, probe_ref, one_ref, other_ref,
     grad_ref, band_ref, side_ref, edge_ref, sum_ref,
-    ext, acc, patch, wave, half, weighted, half2,
+    ext, acc, patch_all, wave_all, half_all, weighted_all, half2_all,
 ):
     rows, cols = own_ref.shape[1:]
     size = probe_ref.shape[-1]
@@ -54,8 +54,9 @@
     per = size // LANES
     lane = lax.broadcasted_iota(jnp.int32, (CHUNK, LANES), 1)
 
-    @pl.loop(0, count_ref[0])
-    def _(slot):
+    bufs = [tuple(ref.at[t] for ref in (patch_all, wave_all, half_all, weighted_all, half2_all)) for t in range(2)]
+
+    def place(slot):
         row = pos_ref[2 * slot]
         col = pos_ref[2 * slot + 1]
         first = col // LANES
@@ -63,6 +64,10 @@
         back_shift = lax.rem(LANES - shift, LANES)
         low = lane < LANES - shift
         high_lanes = lane >= shift
+        return row, first, shift, back_shift, low, high_lanes
+
+    def enter(at, patch, wave):
+        row, first, shift, back_shift, low, high_lanes = at
         for start in range(0, size, CHUNK):
             rs = pl.ds(start, CHUNK)
             obj = []
@@ -80,11 +85,15 @@
                 ms = pl.ds(m * size, size)
                 wave[rs, ms] = (pre * re - pim * im).astype(BF16)
                 wave[pl.ds(size + start, CHUNK), ms] = (pre * im + pim * re).astype(BF16)
+
+    def left_one(wave, half):
         for o in range(2):
             os = pl.ds(o * size, size)
             out = dot(one_ref[os, :], wave[...])
             for m in range(2):
                 half[pl.ds(m * size, size), os] = out[:, m * size : (m + 1) * size].astype(BF16)
+
+    def weigh(slot, live, half, weighted):
         for start in range(0, size, 2 * CHUNK):
             spec = [dot(half[pl.ds(m * size + start, 2 * CHUNK), :], other_ref[...]) for m in range(2)]
             for sub in range(0, 2 * CHUNK, CHUNK):
@@ -92,16 +101,21 @@
                 square = [v[:, :size] * v[:, :size] + v[:, size:] * v[:, size:] for v in s]
                 inv = lax.rsqrt(square[0] + square[1] + 1.0)
                 rs = pl.ds(start + sub, CHUNK)
-                factor = 1.0 - frames_ref[slot, rs, :].astype(F32) * inv
+                factor = live * (1.0 - frames_ref[slot, rs, :].astype(F32) * inv)
                 for m in range(2):
                     for d in range(2):
                         part = s[m][:, d * size : (d + 1) * size] * factor
                         weighted[pl.ds(d * size + start + sub, CHUNK), pl.ds(m * size, size)] = part.astype(BF16)
+
+    def left_other(weighted, half2):
         for o in range(2):
             os = pl.ds(o * size, size)
             out = dot(other_ref[os, :], weighted[...])
             for m in range(2):
                 half2[pl.ds(m * size, size), os] = out[:, m * size : (m + 1) * size].astype(BF16)
+
+    def leave(spot, patch, half2):
+        row, first, shift, back_shift, low, high_lanes = spot
         for start in range(0, size, 2 * CHUNK):
             back = [dot(half2[pl.ds(m * size + start, 2 * CHUNK), :], one_ref[...]) for m in range(2)]
             for sub in range(0, 2 * CHUNK, CHUNK):
@@ -130,6 +144,26 @@
                         here = pl.ds(line(c, first + b, row + at), CHUNK)
                         acc[here, :] += jnp.where(high_lanes, turned[b + 1], turned[b])
 
+    slots = frames_ref.shape[0]
+    count = count_ref[0]
+
+    @pl.loop(0, (count + 1) // 2)
+    def _(step):
+        which = [2 * step, jnp.minimum(2 * step + 1, slots - 1)]
+        alive = [jnp.float32(1.0), (2 * step + 1 < count).astype(F32)]
+        spots = [place(slot) for slot in which]
+        for t in range(2):
+            patch, wave, half, weighted, half2 = bufs[t]
+            enter(spots[t], patch, wave)
+            left_one(wave, half)
+        for t in range(2):
+            patch, wave, half, weighted, half2 = bufs[t]
+            weigh(which[t], alive[t], half, weighted)
+            left_other(weighted, half2)
+        for t in range(2):
+            patch, wave, half, weighted, half2 = bufs[t]
+            leave(spots[t], patch, half2)
+
     for c in range(2):
         for block in range(blocks):
             at = block * LANES
@@ -145,11 +179,69 @@
                 edge_ref[c, :, at : at + LANES] = lower
 
 
+def fetch_kernel(n_row, n_col, own_ref, *refs):
+    local_in, (below_ref, strip_ref, corner_ref) = refs[:4], refs[4:7]
+    own_out, local_out = refs[7], refs[8:12]
+    send_sem, recv_sem, local_sem = refs[12:]
+    i, j = lax.axis_index("row"), lax.axis_index("col")
+    size = strip_ref.shape[2]
+    up, down, left, right = i > 0, i < n_row - 1, j > 0, j < n_col - 1
+    local = [
+        pltpu.make_async_copy(src, dst, local_sem.at[at])
+        for at, (src, dst) in enumerate(zip((own_ref,) + tuple(local_in), (own_out,) + tuple(local_out)))
+    ]
+    barrier = pltpu.get_barrier_semaphore()
+
+    @pl.when(right)
+    def _():
+        pl.semaphore_signal(barrier, inc=1, device_id=(i, j + 1), device_id_type=MESH)
+
+    @pl.when(down)
+    def _():
+        pl.semaphore_signal(barrier, inc=1, device_id=(i + 1, j), device_id_type=MESH)
+
+    @pl.when(left | up)
+    def _():
+        pl.semaphore_wait(barrier, left.astype(jnp.int32) + up.astype(jnp.int32))
+
+    def copy(at, src, dst, to):
+        return pltpu.make_async_remote_copy(
+            src_ref=src, dst_ref=dst, send_sem=send_sem.at[at], recv_sem=recv_sem.at[at], device_id=to, device_id_type=MESH
+        )
+
+    side = copy(0, own_ref.at[:, :, pl.ds(0, size)], strip_ref, (i, j - 1))
+    band = copy(1, own_ref, below_ref, (i - 1, j))
+    edge = copy(2, strip_ref, corner_ref, (i - 1, j))
+    pl.when(left)(side.start)
+    pl.when(up)(band.start)
+    for c in local:
+        c.start()
+
+    def blank(ref):
+        def fill():
+            ref[...] = jnp.zeros_like(ref)
+
+        return fill
+
+    pl.when(jnp.logical_not(right))(blank(strip_ref))
+    pl.when(jnp.logical_not(right & down))(blank(corner_ref))
+    pl.when(jnp.logical_not(down))(blank(below_ref))
+    pl.when(right)(side.wait_recv)
+    pl.when(right & up)(edge.start)
+    for c in local:
+        c.wait()
+    pl.when(down)(band.wait_recv)
+    pl.when(right & down)(edge.wait_recv)
+    pl.when(left)(side.wait_send)
+    pl.when(up)(band.wait_send)
+    pl.when(right & up)(edge.wait_send)
+
+
 def join_kernel(
     n_row, n_col, scale,
     grad_ref, band_ref, side_ref, edge_ref, sum_ref,
     out_ref, probe_ref,
-    band_in, side_in, edge_in, send1, recv1, acc, send2, recv2, acc2, recv3, full2, full1, wide, send_sem, recv_sem,
+    band_in, side_in, edge_in, side_sum, local_sem, send1, recv1, acc, send2, recv2, acc2, recv3, full2, full1, wide, send_sem, recv_sem,
 ):
     i, j = lax.axis_index("row"), lax.axis_index("col")
     size2, size3 = 2 * n_col, n_row // 4
@@ -169,23 +261,23 @@
         return (lax.rem(g3 + d, size3) * 4 + lax.rem(i, 4), j)
 
     has_down, has_up, has_right, has_left = i < n_row - 1, i > 0, j < n_col - 1, j > 0
-    sides = (
-        (has_down, has_up, (i + 1, j), (i - 1, j), band_ref, band_in),
-        (has_right, has_left, (i, j + 1), (i, j - 1), side_ref, side_in),
-        (has_down & has_right, has_up & has_left, (i + 1, j + 1), (i - 1, j - 1), edge_ref, edge_in),
-    )
+    down = (i + 1, j)
     barrier = pltpu.get_barrier_semaphore()
     peers = [partner] + [peer2(d) for d in range(1, size2)] + [peer3(d) for d in range(1, size3)]
     for peer in peers:
         pl.semaphore_signal(barrier, inc=1, device_id=peer, device_id_type=MESH)
-    for _, gets, _, source, _, _ in sides:
-
-        @pl.when(gets)
-        def _():
-            pl.semaphore_signal(barrier, inc=1, device_id=source, device_id_type=MESH)
-
-    targets = sum(sends.astype(jnp.int32) for sends, _, _, _, _, _ in sides)
-    pl.semaphore_wait(barrier, len(peers) + targets)
+
+    @pl.when(has_up)
+    def _():
+        pl.semaphore_signal(barrier, inc=1, device_id=(i - 1, j), device_id_type=MESH)
+
+    @pl.when(has_left)
+    def _():
+        pl.semaphore_signal(barrier, inc=1, device_id=(i, j - 1), device_id_type=MESH)
+
+    start = pltpu.make_async_copy(grad_ref, out_ref, local_sem.at[0])
+    start.start()
+    pl.semaphore_wait(barrier, len(peers) + has_down.astype(jnp.int32) + has_right.astype(jnp.int32))
 
     used = [0]
 
@@ -199,15 +291,20 @@
     send1[...] = sum_ref[pl.ds(pl.multiple_of((1 - k) * n1, n1), n1), :].astype(BF16)
     first = copy(send1, recv1, partner)
     first.start()
-    side_copies = []
-    for sends, gets, to, _, src, dst in sides:
-        c = copy(src, dst, to)
-        side_copies.append(c)
-
-        @pl.when(sends)
-        def _():
-            c.start()
-
+    edge = copy(edge_ref, edge_in, down)
+    side = copy(side_sum, side_in, (i, j + 1))
+    bands = []
+    for at in range(0, band_ref.shape[2], LANES):
+        cut = (slice(None), slice(None), pl.ds(at, LANES))
+        bands.append(copy(band_ref.at[cut], band_in.at[cut], down))
+    waiting = list(bands)
+
+    def release(n):
+        for _ in range(min(n, len(waiting))):
+            pl.when(has_down)(waiting.pop(0).start)
+
+    pl.when(has_down & has_right)(edge.start)
+    release(1)
     first.wait()
     total = sum_ref[pl.ds(pl.multiple_of(k * n1, n1), n1), :] + recv1[...].astype(F32)
     acc[...] = total
@@ -215,6 +312,7 @@
     second = [copy(send2.at[lax.rem(g2 + d, size2)], recv2.at[d - 1], peer2(d)) for d in range(1, size2)]
     for c in second:
         c.start()
+    release(1)
     total = acc[pl.ds(pl.multiple_of(g2 * n2, n2), n2), :]
     for d, c in enumerate(second):
         c.wait()
@@ -223,6 +321,18 @@
     third = [copy(acc2.at[lax.rem(g3 + d, size3)], recv3.at[d - 1], peer3(d)) for d in range(1, size3)]
     for c in third:
         c.start()
+    release(2)
+
+    @pl.when(has_up & has_right)
+    def _():
+        edge.wait_recv()
+        side_sum[...] = (side_ref[...].astype(F32) + edge_in[...].astype(F32)).astype(BF16)
+
+    @pl.when(has_right & jnp.logical_not(has_up))
+    def _():
+        side_sum[...] = side_ref[...]
+
+    pl.when(has_right)(side.start)
     total = acc2[g3]
     for d, c in enumerate(third):
         c.wait()
@@ -231,32 +341,44 @@
     third = [copy(full2.at[g3], full2.at[g3], peer3(d)) for d in range(1, size3)]
     for c in third:
         c.start()
+    release(2)
     for c in third:
         c.wait()
     full1[g2] = full2[...].reshape(n2, LANES).astype(BF16)
     second = [copy(full1.at[g2], full1.at[g2], peer2(d)) for d in range(1, size2)]
     for c in second:
         c.start()
+    release(len(waiting))
     for c in second:
         c.wait()
     wide[k] = full1[...].reshape(n1, LANES)
     last = copy(wide.at[k], wide.at[k], partner)
     last.start()
-    out_ref[...] = grad_ref[...]
-    rows, cols = out_ref.shape[1:]
     size = probe_ref.shape[-1]
-    for (sends, gets, _, _, _, dst), c in zip(sides, side_copies):
-        span = dst.shape[2]
-
-        @pl.when(gets)
-        def _():
+    start.wait()
+
+    @pl.when(has_left)
+    def _():
+        side.wait_recv()
+        out_ref[:, :, :size] += side_in[...].astype(F32)
+
+    @pl.when(has_up)
+    def _():
+        for at, c in enumerate(bands):
             c.wait_recv()
-            out_ref[:, :, :span] += dst[...].astype(F32)
-
-        @pl.when(sends)
-        def _():
+            span = pl.ds(at * LANES, LANES)
+            out_ref[:, :, span] += band_in[:, :, span].astype(F32)
+
+    @pl.when(has_right)
+    def _():
+        side.wait_send()
+
+    @pl.when(has_down)
+    def _():
+        for c in bands:
             c.wait_send()
 
+    pl.when(has_down & has_right)(edge.wait_send)
     last.wait()
     per = size // LANES
     for block in range(4 * per):
@@ -270,15 +392,30 @@
     rows, cols = object_field.shape[1:]
     slots = measured.shape[2]
     one, other = dft_blocks(size)
-    head = object_field[:, :, :size]
-    below = lax.ppermute(object_field, "row", [(i + 1, i) for i in range(n_row - 1)])
-    strip = lax.ppermute(head, "col", [(j + 1, j) for j in range(n_col - 1)])
-    diagonal = [
-        ((i + 1) * n_col + j + 1, i * n_col + j) for i in range(n_row - 1) for j in range(n_col - 1)
-    ]
-    corner = lax.ppermute(head, ("row", "col"), diagonal)
     vmem = pl.BlockSpec(memory_space=pltpu.VMEM)
     smem = pl.BlockSpec(memory_space=pltpu.SMEM)
+    anywhere = pl.BlockSpec(memory_space=pl.ANY)
+    local = (measured[0, 0], probe, one, other)
+    below, strip, corner, own, frames, probe_near, one_near, other_near = pl.pallas_call(
+        functools.partial(fetch_kernel, n_row, n_col),
+        out_shape=[
+            jax.ShapeDtypeStruct((2, size, cols), BF16),
+            jax.ShapeDtypeStruct((2, rows, size), BF16),
+            jax.ShapeDtypeStruct((2, size, size), BF16),
+        ]
+        + [jax.ShapeDtypeStruct(x.shape, x.dtype) for x in (object_field,) + local],
+        in_specs=[pl.BlockSpec(memory_space=pltpu.HBM)] * 5,
+        out_specs=[vmem] * 8,
+        scratch_shapes=[
+            pltpu.SemaphoreType.DMA((3,)),
+            pltpu.SemaphoreType.DMA((3,)),
+            pltpu.SemaphoreType.DMA((5,)),
+        ],
+        compiler_params=pltpu.CompilerParams(
+            collective_id=1, has_side_effects=True, vmem_limit_bytes=44 * 2**20
+        ),
+        name="fetch",
+    )(object_field, *local)
     lines = 4 * size * size // LANES
     work = pl.pallas_call(
         work_kernel,
@@ -294,32 +431,34 @@
         scratch_shapes=[
             pltpu.VMEM((2 * (rows + size) * (cols + size) // LANES, LANES), F32),
             pltpu.VMEM((2 * (rows + size) * (cols + size) // LANES, LANES), F32),
-            pltpu.VMEM((2, size, size), F32),
+            pltpu.VMEM((2, 2, size, size), F32),
         ]
-        + [pltpu.VMEM((2 * size, 2 * size), BF16)] * 4,
-        compiler_params=pltpu.CompilerParams(vmem_limit_bytes=48 * 2**20),
+        + [pltpu.VMEM((2, 2 * size, 2 * size), BF16)] * 4,
+        compiler_params=pltpu.CompilerParams(vmem_limit_bytes=30 * 2**20),
         name="scan",
     )
     grad, band, side, edge, total = work(
-        positions.reshape(-1), counts.reshape(-1), object_field, below, strip, corner, measured[0, 0], probe, one, other
+        positions.reshape(-1), counts.reshape(-1), own, below, strip, corner, frames, probe_near, one_near, other_near
     )
     size2, size3 = 2 * n_col, n_row // 4
     n1 = lines // 2
     n2 = n1 // size2
     n3 = n2 // size3
-    n_copies = 2 + 3 + 2 * (size2 - 1) + 2 * (size3 - 1)
+    n_copies = 2 + 2 + cols // LANES + 2 * (size2 - 1) + 2 * (size3 - 1)
     join = pl.pallas_call(
         functools.partial(join_kernel, n_row, n_col, 1.0 / float(np.sqrt(slots * n_row * n_col))),
         out_shape=[
             jax.ShapeDtypeStruct((2, rows, cols), F32),
             jax.ShapeDtypeStruct(probe.shape, F32),
         ],
-        in_specs=[vmem] * 5,
+        in_specs=[anywhere] + [vmem] * 4,
         out_specs=[vmem] * 2,
         scratch_shapes=[
             pltpu.VMEM(band.shape, BF16),
             pltpu.VMEM(side.shape, BF16),
             pltpu.VMEM(edge.shape, BF16),
+            pltpu.VMEM(side.shape, BF16),
+            pltpu.SemaphoreType.DMA((1,)),
             pltpu.VMEM((n1, LANES), BF16),
             pltpu.VMEM((n1, LANES), BF16),
             pltpu.VMEM((n1, LANES), F32),
@@ -334,7 +473,7 @@
             pltpu.SemaphoreType.DMA((n_copies,)),
         ],
         compiler_params=pltpu.CompilerParams(
-            collective_id=0, has_side_effects=True, vmem_limit_bytes=40 * 2**20
+            collective_id=0, has_side_effects=True, vmem_limit_bytes=18 * 2**20
         ),
         name="join",
     )

time: 90.3 us -> 75.3 us (0.83)
  waiting for transfers between devices: 11.5 us -> 0 us
  starting transfers between devices: 5.17 us -> 0 us
  Pallas kernels: 62.1 us -> 65.8 us
  local copies, waits for them, and re-layouts: 9.98 us -> 7.67 us
    pallas_call x1 -> x2, Pallas kernels: 8.65 us -> 22.7 us  [the longest x1 17.2 us: body(): pl.pallas_call(functools.partial(fetch_kernel, n_row, n_col), out_shape=[...]
    ppermute x3 -> x0, waiting for transfers between devices: 11.5 us -> none  [the longest x1 7.24 us: body(): corner = lax.ppermute(head, ('row', 'col'), diagonal)]
    pallas_call x1, Pallas kernels: 53.5 us -> 43 us  [body(): return tuple(join(grad, band, side, edge, total))]
    ppermute x3 -> x0, starting transfers between devices: 5.17 us -> none  [the longest x1 2.59 us: body(): lax.ppermute(object_field, 'row', [(i + 1, i) for i in range(n_row - 1)])]
    unnamed x13 -> x11, local copies, waits for them, and re-layouts: 8.93 us -> 7.59 us
    slice x1 -> x0, local copies, waits for them, and re-layouts: 0.97 us -> none  [body(): head = object_field[:, :, :size]]
  transfers between devices with their start and end apart: 3 -> 0, of which waited for: 3 -> 0; matrix products, arithmetic and copies ran while one was open for 2% -> 0% of each run, Pallas kernels for 0% -> 0%
where the time goes in v1:
time: 75.3 us; the launch traced here: 74.8 us
  Pallas kernels  65.8 us (87%)
  local copies, waits for them, and re-layouts  7.67 us (10%)
  between operations  1.31 us (2%)
    pallas_call x1, Pallas kernels, body(): return tuple(join(grad, band, side, edge, total))  43 us
    pallas_call x1, Pallas kernels, body(): pl.pallas_call(functools.partial(fetch_kernel, n_row, n_col), out_shape=[...  17.2 us
    unnamed x11, local copies, waits for them, and re-layouts  7.59 us
    pallas_call x1, Pallas kernels, body(): work(positions.reshape(-1), counts.reshape(-1), own, below, strip, corner...  5.54 us

profile of v1, /device:TPU:17, one launch (start us, length us, event | category | flops | bytes accessed | tf_op | source)
XLA Modules:
  0.0 74.8 jit_solution(6370636597591847313)
XLA Ops:
  1.3 0.8 %copy.10 = s32[1,1,12,2]{3,2,1,0:T(8,128)S(1)} copy(s32[1,1,12,2]{2,3,1,0:T(2,128)} %param.10) | data formatting | bytes 192 | tf_op args[3]
  2.0 0.1 reshape.10.pos_ref
  2.1 0.0 copy-start
  2.1 1.2 %copy-done = bf16[2,256,1024]{2,1,0:T(8,128)(2,1)S(1)} copy-done((bf16[2,256,1024]{2,1,0:T(8,128)(2,1)S(1)}, bf16[2,256,1024]{2,1,0:T(8,128)(2,1)}, u32[]{:S(2)}) %copy-start) | copy-done | bytes 1048600
  3.4 0.0 copy-start.1
  3.4 1.2 %copy-done.1 = f32[2,2,256,256]{3,2,1,0:T(8,128)S(1)} copy-done((f32[2,2,256,256]{3,2,1,0:T(8,128)S(1)}, f32[2,2,256,256]{3,2,1,0:T(8,128)}, u32[]{:S(2)}) %copy-start.1) | copy-done | bytes 1048600
  4.6 0.0 copy-start.2
  4.6 1.0 %copy-done.2 = bf16[512,512]{1,0:T(8,128)(2,1)S(1)} copy-done((bf16[512,512]{1,0:T(8,128)(2,1)S(1)}, bf16[512,512]{1,0:T(8,128)(2,1)}, u32[]{:S(2)}) %copy-start.2) | copy-done | bytes 524312
  5.6 0.0 copy-start.3
  5.6 1.0 %copy-done.3 = bf16[512,512]{1,0:T(8,128)(2,1)S(1)} copy-done((bf16[512,512]{1,0:T(8,128)(2,1)S(1)}, bf16[512,512]{1,0:T(8,128)(2,1)}, u32[]{:S(2)}) %copy-start.3) | copy-done | bytes 524312
  6.7 17.2 %fetch.1 = (bf16[2,256,1024]{2,1,0:T(8,128)(2,1)S(1)}, bf16[2,256,256]{2,1,0:T(8,128)(2,1)S(1)}, bf16[2,256,256]{2,1,0:T(8,128)(2,1)S(1)}, bf16[2,256,1024]{2,1,...) custom-call(bf16[2,256,1024]{2,1,0:T(8,128)(2,1)S(1)} %copy-done, ...), custom_call_target="tpu_custom_call" | custom-call | tf_op jit(solution)/shard_map/fetch/pallas_call | solution.py:399
  23.9 5.5 %scan.1 = (f32[2,256,1024]{2,1,0:T(8,128)S(1)}, bf16[2,256,1024]{2,1,0:T(8,128)(2,1)S(1)}, bf16[2,256,256]{2,1,0:T(8,128)(2,1)S(1)}, bf16[2,256,256]{2,1,0:T(8,128)(2,1)S(1)}, f32[2048,128]{1,0:T(8,128)S(1)}) custom-call(s32[24]{0:T(128)S(1)} %reshape.10.pos_ref, s32[1]{0:T(128)} %bitcast.2.count_ref, bf16[2,256,1024]{2,1,0:T(8,128)(2,1)S(1)} %get-tuple-element.15.own_ref, ...), custom_call_target="tpu_custom_call" | custom-call | tf_op jit(solution)/shard_map/scan/pallas_call | solution.py:440
  29.4 43.0 %join.1 = (f32[2,256,1024]{2,1,0:T(8,128)S(1)}, f32[2,2,256,256]{3,2,1,0:T(8,128)S(1)}) custom-call(f32[2,256,1024]{2,1,0:T(8,128)S(1)} %get-tuple-element.23.grad_ref, bf16[2,256,1024]{2,1,0:T(8,128)(2,1)S(1)} %get-tuple-element.24.band_ref, bf16[2,256,256]{2,1,0:T(8,128)(2,1)S(1)} %get-tuple-element.25.side_ref, ...), custom_call_target="tpu_custom_call" | custom-call | tf_op jit(solution)/shard_map/join/pallas_call | solution.py:480
  72.5 1.3 %copy.14 = f32[2,256,1024]{2,1,0:T(8,128)} copy(f32[2,256,1024]{2,1,0:T(8,128)S(1)} %get-tuple-element.30) | data formatting | bytes 4194304
  73.8 1.0 %copy.15 = f32[2,2,256,256]{3,2,1,0:T(8,128)} copy(f32[2,2,256,256]{3,2,1,0:T(8,128)S(1)} %get-tuple-element.31) | data formatting | bytes 2097152
Async XLA Ops:
  2.1 1.2 %copy-start = (bf16[2,256,1024]{2,1,0:T(8,128)(2,1)S(1)}, bf16[2,256,1024]{2,1,0:T(8,128)(2,1)}, u32[]{:S(2)}) copy-start(bf16[2,256,1024]{2,1,0:T(8,128)(2,1)} %own_ref.1) | copy-start | bytes 3145732
  3.4 1.2 %copy-start.1 = (f32[2,2,256,256]{3,2,1,0:T(8,128)S(1)}, f32[2,2,256,256]{3,2,1,0:T(8,128)}, u32[]{:S(2)}) copy-start(f32[2,2,256,256]{3,2,1,0:T(8,128)} %refs_1_.1) | copy-start | bytes 3145732
  4.6 1.0 %copy-start.2 = (bf16[512,512]{1,0:T(8,128)(2,1)S(1)}, bf16[512,512]{1,0:T(8,128)(2,1)}, u32[]{:S(2)}) copy-start(bf16[512,512]{1,0:T(8,128)(2,1)} %constant.10.refs_3_) | copy-start | bytes 1572868
  5.6 1.0 %copy-start.3 = (bf16[512,512]{1,0:T(8,128)(2,1)S(1)}, bf16[512,512]{1,0:T(8,128)(2,1)}, u32[]{:S(2)}) copy-start(bf16[512,512]{1,0:T(8,128)(2,1)} %constant.9.refs_2_) | copy-start | bytes 1572868
